TPU v7x, 256 devices: a whole 4x4x8 slice. The times are simulated.
256 devices in a mesh: seg: 8 (over y, core), op: 32 (over x, z).
Axes of the slice: x: 4, y: 4, z: 8, core: 2. Of those that a mesh axis runs over, the one named last changes fastest.
Arguments:
- left_ops: float32 [8, 32, 768, 768], P('seg', 'op'), as said below
- right_ops: float32 [8, 32, 768, 768], P('seg', 'op'), as said below
- wavefunction: float32 [8, 768, 768], P('seg', 'op'), as said below
- basis_rotation: float32 [8, 768, 768], P('seg'), may hold values from -0.21875 to 0.21875
- pair_term: int32 [8, 32], P('seg', 'op'), may hold values from 0 to 15
- coupling: float32 [16], replicated, may hold values from 0.1 to 1
- left_charge: int32 [8, 768], P('seg'), may hold values from 0 to 2, as said below
- right_charge: int32 [8, 768], P('seg'), may hold values from 0 to 2, as said below
Outputs:
- chebyshev: float32 [8, 768, 768], P('seg', 'op')
- energy: float32 [8], P('seg')
- handed: float32 [8, 32, 768, 768], P('seg', 'op')
Inputs may be any that keep to these rules, and one draw needn't show every extreme that they name: `left_ops`: each operator is a dominant positive diagonal plus dense full-rank off-diagonal entries. `right_ops`: each operator is a dominant positive diagonal plus dense full-rank off-diagonal entries. `wavefunction`: dense real entries of varying scale. `left_charge`: in each segment exactly 256 left bond states carry each quantum number. `right_charge`: in each segment exactly 256 right bond states carry each quantum number.
All inputs are finite; a program needn't handle non-finite values.
Results may differ from a plain program's by a relative error of at most 0.0003.
Values sent between devices are 32-bit elements; how exact they have to be, the bound alone decides.
A program may use at most 128 MiB of HBM per device.

v0:
```python
import jax
import jax.numpy as jnp
from jax import lax
from jax.sharding import PartitionSpec as P

HIGH = lax.Precision.HIGHEST


def passed_along(value, axis, steps):
    count = lax.axis_size(axis)
    first, last = (max(0, -steps), min(count, count - steps))
    return lax.ppermute(value, axis, [(source, source + steps) for source in range(first, last)])


def local_terms(vector, left_ops, right_ops, coefficient):
    partial_value = jnp.einsum("kab,bc->kac", left_ops, vector, precision=HIGH)
    partial_value = partial_value * coefficient[:, None, None]
    return jnp.einsum("kac,kcd->ad", partial_value, right_ops, precision=HIGH)


def per_device(
    left_ops,
    right_ops,
    wavefunction,
    basis_rotation,
    pair_term,
    coupling,
    left_charge,
    right_charge,
):
    own_left = left_ops[0]
    own_right = right_ops[0]
    row_count = wavefunction.shape[1]
    full_size = wavefunction.shape[2]
    width = float(full_size * full_size)
    row_start = lax.axis_index("op") * row_count
    sector_mask = (left_charge[0][:, None] == right_charge[0][None, :]).astype(jnp.float32)
    table_hits = (
        pair_term[0][:, None] == jnp.arange(coupling.shape[0], dtype=jnp.int32)[None, :]
    ).astype(jnp.float32)
    coefficient = jnp.sum(table_hits * coupling[None, :], axis=1)
    gathered = lax.all_gather(wavefunction, "op", axis=1, tiled=True)[0]
    masked = sector_mask * gathered
    initial = masked / jnp.sqrt(jnp.sum(masked * masked) / width + 1e-06)

    def full_apply(vector):
        partial_value = local_terms(vector, own_left, own_right, coefficient) * sector_mask
        return lax.psum(partial_value, "op")

    image_one = full_apply(initial)
    energy = jnp.sum(initial * image_one) / width
    spread = jnp.sqrt(jnp.sum(image_one * image_one) / width + 1e-06)
    first_step = (image_one - energy * initial) / spread
    image_two = full_apply(first_step)
    whole_result = 2.0 * (image_two - energy * first_step) / spread - initial
    chebyshev = lax.dynamic_slice_in_dim(whole_result, row_start, row_count, 0)
    half_turn = jnp.einsum("kab,bj->kaj", own_left, basis_rotation[0], precision=HIGH)
    rotated = jnp.einsum("ai,kaj->kij", basis_rotation[0], half_turn, precision=HIGH)
    shifted = passed_along(rotated, "seg", 1)
    handed = jnp.where(lax.axis_index("seg") == 0, own_left, shifted)
    return (chebyshev[None], jnp.reshape(energy, (1,)), handed[None])


def solution(mesh):
    placed = (
        P("seg", "op", None, None),
        P("seg", "op", None, None),
        P("seg", "op", None),
        P("seg", None, None),
        P("seg", "op"),
        P(),
        P("seg", None),
        P("seg", None),
    )
    return jax.shard_map(
        per_device,
        mesh=mesh,
        in_specs=placed,
        out_specs=(P("seg", "op", None), P("seg"), P("seg", "op", None, None)),
        check_vma=False,
    )
```

profile of v0, /device:TPU:8, one launch (start us, length us, event | category | flops | bytes accessed | tf_op | source)
XLA Modules:
  0.0 460.7 jit_solution(3660629556880406325)
XLA Ops:
  7.2 0.0 copy-start
  7.2 0.0 all-gather.2.cloned.1.call-start
  7.2 0.7 all-gather.2.cloned.1.call-update
  7.9 0.0 all-reduce.3.cloned.1.call-start
  8.0 0.7 reduce.2
  8.7 0.7 reduce.3
  10.0 1.3 fusion.41
  11.3 80.5 %all-gather.2.cloned.1.call-done = f32[1,768,768]{2,1,0:T(8,128)} async-done(((f32[1,24,768]{2,1,0:T(8,128)}), f32[1,768,768]{2,1,0:T(8,128)}) %all-gather.2.cloned.1.call-update) | async-done | bytes 2359312 | tf_op jit(solution)/shard_map/all_gather | solution.py:42
  91.8 3.0 multiply_reduce_fusion.2
  95.4 0.0 copy-start.3
  95.4 14.1 %fusion.12 = f32[768,768]{1,0:T(8,128)S(1)} fusion(f32[1,1,768,768]{3,2,1,0:T(8,128)} %param.8, f32[1,768,768]{2,1,0:T(8,128)} %all-gather.2.cloned.1.call-done, f32[]{:T(128)S(6)} %sqrt.6, s32[768]{0:T(1024)S(1)} %reduce.3, s32[768]{0:T(1024)S(1)} %reduce.2), kind=kOutput, calls=%fused_computation.16 | convolution fusion | flops 5437587456 | bytes 7084036 | tf_op jit(solution)/shard_map/kab,bc->kac/dot_general | solution.py:16
  109.6 8.1 %compare_select_fusion.1 = f32[768,768]{1,0:T(8,128)} fusion(f32[1,1,768,768]{3,2,1,0:T(8,128)S(1)} %copy-done.3, f32[768,768]{1,0:T(8,128)S(1)} %fusion.12, f32[]{:T(128)} %fusion.41, s32[768]{0:T(1024)S(1)} %reduce.3, s32[768]{0:T(1024)S(1)} %reduce.2), kind=kOutput, calls=%fused_computation.1 | convolution fusion | flops 5437587456 | bytes 7084036 | tf_op jit(solution)/shard_map/kac,kcd->ad/dot_general | solution.py:18
  117.6 0.0 all-reduce.3.cloned.1.call-update
  117.7 0.0 all-reduce.5.cloned.1.call-start
  117.7 7.6 %fusion.2 = f32[768,768]{1,0:T(8,128)S(1)} fusion(f32[1,768,768]{2,1,0:T(8,128)S(1)} %copy-done, f32[1,1,768,768]{3,2,1,0:T(8,128)} %param.8), kind=kOutput, calls=%fused_computation.5 | convolution fusion | flops 5435817984 | bytes 7077888 | tf_op jit(solution)/shard_map/kab,bj->kaj/dot_general | solution.py:57
  125.4 7.7 %fusion.29 = f32[1,768,768]{1,2,0:T(8,128)} fusion(f32[768,768]{1,0:T(8,128)S(1)} %fusion.2, f32[1,768,768]{2,1,0:T(8,128)S(1)} %copy-done), kind=kOutput, calls=%fused_computation.29 | convolution fusion | flops 5435817984 | bytes 7077888 | tf_op jit(solution)/shard_map/ai,kaj->kij/dot_general | solution.py:58
  133.1 2.3 collective-permute-start
  135.4 134.4 %all-reduce.3.cloned.1.call-done = f32[768,768]{1,0:T(8,128)} async-done(((f32[768,768]{1,0:T(8,128)}), f32[768,768]{1,0:T(8,128)}) %all-reduce.3.cloned.1.call-update) | async-done | bytes 2359312 | tf_op jit(solution)/shard_map/psum | solution.py:48
  269.9 4.8 %multiply_reduce_fusion.1 = (f32[]{:T(128)}, f32[]{:T(128)}, f32[768,768]{1,0:T(8,128)}) fusion(f32[768,768]{1,0:T(8,128)} %all-reduce.3.cloned.1.call-done, f32[]{:T(128)S(6)} %sqrt.6, f32[1,768,768]{2,1,0:T(8,128)} %all-gather.2.cloned.1.call-done, s32[768]{0:T(1024)S(1)} %reduce.3, s32[768]{0:T(1024)S(1)} %reduce.2), kind=kLoop, calls=%fused_computation.22 | loop fusion | flops 4128766 | bytes 7084044 | tf_op jit(solution)/shard_map/reduce_sum | solution.py:51
  276.0 0.0 copy-start.1
  276.0 2.8 subtract_divide_fusion
  278.9 0.2 copy-done.1
  279.1 11.7 %fusion.10 = f32[768,768]{1,0:T(8,128)S(1)} fusion(f32[768,768]{1,0:T(8,128)S(1)} %subtract_divide_fusion, f32[1,1,768,768]{3,2,1,0:T(8,128)S(1)} %copy-done.1), kind=kOutput, calls=%fused_computation.14 | convolution fusion | flops 5435817984 | bytes 7077888 | tf_op jit(solution)/shard_map/kab,bc->kac/dot_general | solution.py:16
  290.8 0.0 copy-done.2
  290.9 8.2 %compare_select_fusion = f32[768,768]{1,0:T(8,128)} fusion(f32[1,1,768,768]{3,2,1,0:T(8,128)S(1)} %copy-done.4, f32[768,768]{1,0:T(8,128)S(1)} %fusion.10, f32[]{:T(128)} %fusion.41, s32[768]{0:T(1024)S(1)} %reduce.3, s32[768]{0:T(1024)S(1)} %reduce.2), kind=kOutput, calls=%fused_computation | convolution fusion | flops 5437587456 | bytes 7084036 | tf_op jit(solution)/shard_map/kac,kcd->ad/dot_general | solution.py:18
  299.0 0.0 all-reduce.5.cloned.1.call-update
  299.1 3.0 copy.11
  302.1 0.0 collective-permute-done
  302.1 4.1 fusion.4
  306.2 3.2 copy.12
  309.4 141.9 %all-reduce.5.cloned.1.call-done = f32[768,768]{1,0:T(8,128)} async-done(((f32[768,768]{1,0:T(8,128)}), f32[768,768]{1,0:T(8,128)}) %all-reduce.5.cloned.1.call-update) | async-done | bytes 2359312 | tf_op jit(solution)/shard_map/psum | solution.py:48
  451.3 1.6 fusion.38
  (5 shorter events, 0.0 us)
Async XLA Ops:
  7.2 110.5 %copy-start = (f32[1,768,768]{2,1,0:T(8,128)S(1)}, f32[1,768,768]{2,1,0:T(8,128)}, u32[]{:S(2)}) copy-start(f32[1,768,768]{2,1,0:T(8,128)} %param.11) | copy-start | bytes 7077892
  7.2 84.6 %all-gather.2.cloned.1.call-start = ((), (), s32[]{:S(2)}) async-start(), calls=%async_computation | async-start | bytes 2433024 | tf_op jit(solution)/shard_map/all_gather | solution.py:42
  7.9 261.9 %all-reduce.3.cloned.1.call-start = ((), (), s32[]{:S(2)}) async-start(), calls=%async_computation.1 | async-start | bytes 4718592 | tf_op jit(solution)/shard_map/psum | solution.py:48
  95.4 14.1 %copy-start.3 = (f32[1,1,768,768]{3,2,1,0:T(8,128)S(1)}, f32[1,1,768,768]{3,2,1,0:T(8,128)}, u32[]{:S(2)}) copy-start(f32[1,1,768,768]{3,2,1,0:T(8,128)} %param.9) | copy-start | bytes 7077892
  117.7 333.6 %all-reduce.5.cloned.1.call-start = ((), (), s32[]{:S(2)}) async-start(), calls=%async_computation.2 | async-start | bytes 4718592 | tf_op jit(solution)/shard_map/psum | solution.py:48
  133.1 169.0 %collective-permute-start = (f32[1,768,768]{1,2,0:T(8,128)}, f32[1,768,768]{1,2,0:T(8,128)}, u32[]{:S(2)}, u32[]{:S(2)}) collective-permute-start(f32[1,768,768]{1,2,0:T(8,128)} %fusion.29), channel_id=1, source_target_pairs={{0,32},{32,64},{64,96},{96,128},{128,160},{160,192},{192,224},{1,3... | collective-permute-start | bytes 7077896 | tf_op jit(solution)/shard_map/ppermute | solution.py:12
  276.0 3.1 copy-start.1
  279.1 11.7 %copy-start.2 = (f32[768,768]{1,0:T(8,128)}, f32[768,768]{1,0:T(8,128)S(1)}, u32[]{:S(2)}) copy-start(f32[768,768]{1,0:T(8,128)S(1)} %subtract_divide_fusion) | copy-start | bytes 7077892
  279.1 11.7 %copy-start.4 = (f32[1,1,768,768]{3,2,1,0:T(8,128)S(1)}, f32[1,1,768,768]{3,2,1,0:T(8,128)}, u32[]{:S(2)}) copy-start(f32[1,1,768,768]{3,2,1,0:T(8,128)} %param.9) | copy-start | bytes 7077892
Sparse Core Ops, SparseCore 0:
  10.6 81.1 all-gather.1
  117.8 152.0 all-reduce.2
  299.2 152.0 all-reduce.4
where the time goes:
time: 470 us; the launch traced here: 461 us
  waiting for transfers between devices  358 us (76%)
  matrix products  57.4 us (12%)
  other arithmetic  18.9 us (4%)
  between operations  17.9 us (4%)
  local copies, waits for them, and re-layouts  6.55 us (1%)
    psum x2, waiting for transfers between devices, full_apply(): return lax.psum(partial_value, 'op')  276 us
    all_gather x1, waiting for transfers between devices, per_device(): gathered = lax.all_gather(wavefunction, 'op', axis=1, tiled=True)[0]  80.5 us
    dot_general x2, matrix products, local_terms(): partial_value = jnp.einsum('kab,bc->kac', left_ops, vector, precision=HIGH)  25.8 us
    dot_general x2, matrix products, local_terms(): return jnp.einsum('kac,kcd->ad', partial_value, right_ops, precision=HIGH)  16.3 us
  transfers between devices with their start and end apart: 4, of which 3 were waited for; matrix products, arithmetic and copies ran while one was open for 12% of the time, Pallas kernels for 0%

commit v1 on v0

v1 whole, which is shorter than its diff:
```python
import functools
import jax
import jax.numpy as jnp
from jax import lax
from jax.experimental import pallas as pl
from jax.experimental.pallas import tpu as pltpu
from jax.sharding import PartitionSpec as P

MESH = pl.DeviceIdType.MESH
F32, BF16 = jnp.float32, jnp.bfloat16
NX, NZ = 4, 8
SECTORS = 3
M = 768
Q = M // SECTORS
ROWS = 8
OPS = NX * NZ
NN = (((1,), (0,)), ((), ()))
NT = (((1,), (1,)), ((), ()))


def dot(a, b, dims=NN):
    return lax.dot_general(a, b, dims, preferred_element_type=F32)


def dot3(a_high, a_low, b_high, b_low):
    return dot(a_high, b_high) + (dot(a_high, b_low) + dot(a_low, b_high))


def halves(value):
    high = value.astype(BF16)
    low = (value - high.astype(F32)).astype(BF16)
    return high, low


def thirds(value):
    high = value.astype(BF16)
    rest = value - high.astype(F32)
    middle = rest.astype(BF16)
    low = (rest - middle.astype(F32)).astype(BF16)
    return high, middle, low


def peer(dx, dz):
    op = lax.axis_index("op")
    x, z = op // NZ, op % NZ
    return lax.rem(x + dx, NX) * NZ + lax.rem(z + dz, NZ)


def remote(source, target, send, receive, device):
    copy = pltpu.make_async_remote_copy(
        source, target, send, receive, device_id=device, device_id_type=MESH
    )
    copy.start()
    return copy


def kernel(
    left_hbm, right_hbm, basis_hbm, wave_ref, left_charge_ref, right_charge_ref, term_ref, coupling_ref,
    cheb_ref, energy_ref, handed_hbm,
    left, right, basis, load_sem,
    left_high, left_low, right_high, right_low,
    basis_high, basis_low, turned_high, turned_low, half_high, half_low, rotated,
    to_left, to_right, from_left, position_column,
    scratch_high, scratch_low, y_high, y_low, x_high, x_low,
    initial, first, gather_one, gather_two, partial_one, partial_two,
    land_one, land_two, middle_one, middle_two, final_one, final_two,
    send_sems, recv_sems, hand_send, hand_recv, own_sem,
):
    seg, op = lax.axis_index("seg"), lax.axis_index("op")
    x, z = op // NZ, op % NZ
    width = float(M * M)

    loads = [
        pltpu.make_async_copy(source, target, load_sem.at[i])
        for i, (source, target) in enumerate(((right_hbm, right), (left_hbm, left), (basis_hbm, basis)))
    ]
    for load in loads:
        load.start()
    barrier = pltpu.get_barrier_semaphore()
    for dx in range(1, NX):
        pl.semaphore_signal(barrier, inc=1, device_id={"op": peer(dx, 0)}, device_id_type=MESH)
    for dz in range(1, NZ):
        pl.semaphore_signal(barrier, inc=1, device_id={"op": peer(0, dz)}, device_id_type=MESH)
    segs = lax.axis_size("seg")
    for ds in (1, segs - 1):
        pl.semaphore_signal(barrier, inc=1, device_id={"seg": lax.rem(seg + ds, segs)}, device_id_type=MESH)

    before = lax.broadcasted_iota(jnp.int32, (M, M), 0) < lax.broadcasted_iota(jnp.int32, (M, M), 1)
    to_left[...] = jnp.where(before, 1.0, 0.0).astype(BF16)
    sector = lax.broadcasted_iota(jnp.int32, (8, M), 0)
    left_hits = jnp.where(left_charge_ref[...] == sector, 1.0, 0.0)
    right_hits = jnp.where(right_charge_ref[...] == sector, 1.0, 0.0)
    counts = dot(jnp.concatenate([left_hits, right_hits], 0).astype(BF16), to_left[...])
    left_rank = jnp.sum(left_hits * counts[:8], 0, keepdims=True)
    right_rank = jnp.sum(right_hits * counts[8:], 0, keepdims=True)
    left_place = left_charge_ref[...] * Q + left_rank.astype(jnp.int32)
    right_place = right_charge_ref[...] * Q + right_rank.astype(jnp.int32)
    place = lax.broadcasted_iota(jnp.int32, (M, M), 0)
    to_right[...] = jnp.where(place == right_place, 1.0, 0.0).astype(BF16)
    position_column[...] = jnp.transpose(jnp.broadcast_to(left_place.astype(F32), (128, M)))

    own_position = position_column[pl.ds(pl.multiple_of(op * 24, 8), 24), 0:1]
    moved = sum(dot(part, to_right[...], NT) for part in thirds(wave_ref[...]))
    own_rows = jnp.where(
        own_position < Q, moved[:, :Q], jnp.where(own_position < 2 * Q, moved[:, Q : 2 * Q], moved[:, 2 * Q :])
    )
    for p in range(SECTORS):
        gather_one[p, x, z] = own_rows[p * ROWS : (p + 1) * ROWS]

    pl.semaphore_wait(barrier, NX + NZ)

    def along(axis, phase, p, level, source, target):
        copies = []
        for d in range(1, NX if axis == "x" else NZ):
            far = lax.rem(x + d, NX) if axis == "x" else lax.rem(z + d, NZ)
            device = peer(d, 0) if axis == "x" else peer(0, d)
            copies.append(
                remote(
                    source(far), target(d),
                    send_sems.at[phase, p, level, d], recv_sems.at[phase, p, level, d], {"op": device},
                )
            )
        return copies

    sent = []

    def arrived(copies):
        for copy in copies:
            copy.wait_recv()
        sent.extend(copies)

    def gather_near(phase, buffer, p):
        ref = buffer.at[p, x, z]
        return along("x" if p == 0 else "z", phase, p, 0, lambda far: ref, lambda d: ref)

    def gather_far(phase, buffer, p):
        ref = buffer.at[p, :, z] if p == 0 else buffer.at[p, x]
        return along("z" if p == 0 else "x", phase, p, 1, lambda far: ref, lambda d: ref)

    def scatter_far(phase, partial, land, p):
        if p == 0:
            return along("z", phase, p, 0, lambda far: partial.at[p, :, far], lambda d: land[0].at[d])
        return along("x", phase, p, 0, lambda far: partial.at[p, far], lambda d: land[1].at[p - 1, d])

    def scatter_near(phase, partial, land, middle, final, p):
        if p == 0:
            middle[0][...] = partial[p, :, z] + sum(land[0][d] for d in range(1, NZ))
            return along("x", phase, p, 1, lambda far: middle[0].at[far], lambda d: final[0].at[d])
        middle[1][p - 1] = partial[p, x] + sum(land[1][p - 1, d] for d in range(1, NX))
        return along("z", phase, p, 1, lambda far: middle[1].at[p - 1, far], lambda d: final[1].at[p - 1, d])

    def scattered(middle, final, p):
        if p == 0:
            return middle[0][x] + sum(final[0][d] for d in range(1, NX))
        return middle[1][p - 1, z] + sum(final[1][p - 1, d] for d in range(1, NZ))

    def split(source, high, low):
        @pl.loop(0, SECTORS)
        def _(i):
            rows = pl.ds(pl.multiple_of(i * Q, Q), Q)
            high[rows, :], low[rows, :] = halves(source[rows, :])

    def sort_columns(source, order, high, low):
        @pl.loop(0, SECTORS)
        def _(i):
            rows = pl.ds(pl.multiple_of(i * Q, Q), Q)
            part_high, part_low = halves(source[rows, :])
            high[rows, :] = dot(part_high, order[...], NT).astype(BF16)
            low[rows, :] = dot(part_low, order[...], NT).astype(BF16)

    def sort_rows(order, source_high, source_low, high, low):
        @pl.loop(0, SECTORS)
        def _(i):
            rows = pl.ds(pl.multiple_of(i * Q, Q), Q)
            high[rows, :] = dot(order[rows, :], source_high[...]).astype(BF16)
            low[rows, :] = dot(order[rows, :], source_low[...]).astype(BF16)

    def first_turn():
        @pl.loop(0, SECTORS)
        def _(i):
            rows = pl.ds(pl.multiple_of(i * Q, Q), Q)
            part_high, part_low = halves(left[rows, :])
            value = dot3(part_high, part_low, basis_high[...], basis_low[...])
            half_high[rows, :], half_low[rows, :] = halves(value)

    def second_turn():
        for i in range(SECTORS):
            rows = pl.ds(i * Q, Q)
            rotated[rows, :] = dot3(turned_high[rows, :], turned_low[rows, :], half_high[...], half_low[...])

            @pl.when(seg < segs - 1)
            def _():
                hand(i).start()

    def hand(i):
        rows = pl.ds(i * Q, Q)
        return pltpu.make_async_remote_copy(
            rotated.at[rows, :], handed_hbm.at[rows, :], hand_send.at[i], hand_recv.at[i],
            device_id={"seg": lax.rem(seg + 1, segs)}, device_id_type=MESH,
        )

    def transpose_basis():
        for i in range(M // 128):
            cols = pl.ds(i * 128, 128)
            turned_high[:, cols], turned_low[:, cols] = halves(jnp.transpose(basis[cols, :]))

    coefficient = coupling_ref[term_ref[0, 0]]

    def inner(p):
        rows = pl.ds(p * Q, Q)
        value = coefficient * dot3(left_high[:, rows], left_low[:, rows], x_high[rows, :], x_low[rows, :])
        y_high[:, rows], y_low[:, rows] = halves(value)

    def outer(p):
        rows = pl.ds(p * Q, Q)
        return dot3(y_high[rows, :], y_low[rows, :], right_high[:, rows], right_low[:, rows])

    near = [gather_near(0, gather_one, p) for p in range(SECTORS)]

    to_left[...] = jnp.where(place == left_place, 1.0, 0.0).astype(BF16)
    loads[0].wait()
    sort_columns(right, to_right, scratch_high, scratch_low)

    far = []
    for p in range(SECTORS):
        arrived(near[p])
        far.append(gather_far(0, gather_one, p))

    sort_rows(to_right, scratch_high, scratch_low, right_high, right_low)
    loads[1].wait()

    @pl.when(seg == 0)
    def _():
        pltpu.make_async_copy(left, handed_hbm, own_sem).start()

    sort_columns(left, to_left, scratch_high, scratch_low)
    sort_rows(to_left, scratch_high, scratch_low, left_high, left_low)
    lane = lax.broadcasted_iota(jnp.int32, (M, 128), 1).astype(F32)
    for i in range(M // 128):
        hits = position_column[...] == lane + float(i * 128)
        from_left[:, i * 128 : (i + 1) * 128] = jnp.where(hits, 1.0, 0.0).astype(BF16)

    for p in range(SECTORS):
        arrived(far[p])

    whole = gather_one[...].reshape(SECTORS, OPS, ROWS, Q)
    masked = jnp.stack([whole[p] for p in range(SECTORS)], 1).reshape(M, Q)
    scale = jnp.sqrt(jnp.sum(masked * masked) / width + 1e-06)
    masked_high, masked_low = halves(masked / scale)
    sorted_high = dot(to_left[...], masked_high)
    sorted_low = dot(to_left[...], masked_low)
    x_high[...] = sorted_high.astype(BF16)
    x_low[...] = sorted_low.astype(BF16)
    initial[...] = sorted_high + sorted_low
    own_initial = own_rows / scale

    for p in range(SECTORS):
        inner(p)
    far = []
    for p in range(SECTORS):
        partial_one[p] = outer(p).reshape(NX, NZ, ROWS, Q)
        far.append(scatter_far(1, partial_one, land_one, p))

    loads[2].wait()
    split(basis, basis_high, basis_low)
    first_turn()

    near = [None] * SECTORS
    for p in (1, 0, 2):
        arrived(far[p])
        near[p] = scatter_near(1, partial_one, land_one, middle_one, final_one, p)

    transpose_basis()

    far = [None] * SECTORS
    for p in (1, 0, 2):
        arrived(near[p])
        gather_two[p, x, z] = scattered(middle_one, final_one, p)
        far[p] = gather_near(2, gather_two, p)

    second_turn()

    last = [None] * SECTORS
    for p in (1, 0, 2):
        arrived(far[p])
        last[p] = gather_far(2, gather_two, p)
    for p in range(SECTORS):
        arrived(last[p])

    image = gather_two[...].reshape(M, Q)
    start = initial[...]
    energy = jnp.sum(start * image) / width
    spread = jnp.sqrt(jnp.sum(image * image) / width + 1e-06)
    energy_ref[0] = energy
    step = (image - energy * start) / spread
    first[...] = step
    x_high[...], x_low[...] = halves(step)
    for p in range(SECTORS):
        inner(p)
    for p in range(SECTORS):
        out_high, out_low = halves(outer(p))
        rows = pl.ds(p * Q, Q)
        y_high[rows, 0:Q] = out_high
        y_low[rows, 0:Q] = out_low
    back = dot(from_left[...], y_high[:, 0:Q]) + dot(from_left[...], y_low[:, 0:Q])
    back = back.reshape(OPS, SECTORS, ROWS, Q)
    far = []
    for p in range(SECTORS):
        partial_two[p] = back[:, p].reshape(NX, NZ, ROWS, Q)
        far.append(scatter_far(3, partial_two, land_two, p))

    own_select = jnp.where(
        own_position == lax.broadcasted_iota(jnp.int32, (24, M), 1).astype(F32), 1.0, 0.0
    ).astype(BF16)
    own_step = sum(dot(own_select, part) for part in thirds(first[...]))

    near = [None] * SECTORS
    for p in (1, 0, 2):
        arrived(far[p])
        near[p] = scatter_near(3, partial_two, land_two, middle_two, final_two, p)
    own_image = []
    for p in range(SECTORS):
        arrived(near[p])
        own_image.append(scattered(middle_two, final_two, p))
    own_image = jnp.concatenate(own_image, 0)
    result = 2.0 * (own_image - energy * own_step) / spread - own_initial
    spread_out = jnp.concatenate(
        [
            jnp.where((own_position >= p * Q) & (own_position < (p + 1) * Q), result, 0.0)
            for p in range(SECTORS)
        ],
        1,
    )
    cheb_ref[...] = sum(dot(part, to_right[...]) for part in thirds(spread_out))

    for copy in sent:
        copy.wait_send()

    @pl.when(seg == 0)
    def _():
        pltpu.make_async_copy(left, handed_hbm, own_sem).wait()

    @pl.when(seg < segs - 1)
    def _():
        for i in range(SECTORS):
            hand(i).wait_send()

    @pl.when(seg > 0)
    def _():
        for i in range(SECTORS):
            hand(i).wait_recv()


def per_device(
    left_ops,
    right_ops,
    wavefunction,
    basis_rotation,
    pair_term,
    coupling,
    left_charge,
    right_charge,
):
    vmem, smem, hbm = (
        pl.BlockSpec(memory_space=space) for space in (pltpu.VMEM, pltpu.SMEM, pl.ANY)
    )
    dma = pltpu.SemaphoreType.DMA

    def full(dtype):
        return pltpu.VMEM((M, M), dtype)

    def parts():
        return pltpu.VMEM((SECTORS, NX, NZ, ROWS, Q), F32)

    def tall(dtype):
        return pltpu.VMEM((M, Q), dtype)

    land = [pltpu.VMEM((NZ, NX, ROWS, Q), F32), pltpu.VMEM((2, NX, NZ, ROWS, Q), F32)]
    middle = [pltpu.VMEM((NX, ROWS, Q), F32), pltpu.VMEM((2, NZ, ROWS, Q), F32)]
    final = [pltpu.VMEM((NX, ROWS, Q), F32), pltpu.VMEM((2, NZ, ROWS, Q), F32)]
    cheb, energy, handed = pl.pallas_call(
        kernel,
        name="segment_step",
        out_shape=(
            jax.ShapeDtypeStruct((24, M), F32),
            jax.ShapeDtypeStruct((1,), F32),
            jax.ShapeDtypeStruct((M, M), F32),
        ),
        in_specs=[hbm, hbm, hbm, vmem, vmem, vmem, smem, smem],
        out_specs=(vmem, smem, hbm),
        scratch_shapes=[
            full(F32), full(F32), full(F32), dma((3,)),
            full(BF16), full(BF16), full(BF16), full(BF16),
            full(BF16), full(BF16), full(BF16), full(BF16), full(BF16), full(BF16), full(F32),
            full(BF16), full(BF16), full(BF16), pltpu.VMEM((M, 128), F32),
            full(BF16), full(BF16), full(BF16), full(BF16), tall(BF16), tall(BF16),
            tall(F32), tall(F32), parts(), parts(), parts(), parts(),
            list(land), list(land), list(middle), list(middle), list(final), list(final),
            dma((4, SECTORS, 2, NZ)), dma((4, SECTORS, 2, NZ)), dma((SECTORS,)), dma((SECTORS,)), dma,
        ],
        compiler_params=pltpu.CompilerParams(
            collective_id=0, has_side_effects=True, vmem_limit_bytes=58 * 2**20
        ),
    )(
        left_ops[0, 0], right_ops[0, 0], basis_rotation[0], wavefunction[0],
        left_charge, right_charge, pair_term, coupling,
    )
    return cheb[None], energy, handed[None, None]


def solution(mesh):
    placed = (
        P("seg", "op", None, None),
        P("seg", "op", None, None),
        P("seg", "op", None),
        P("seg", None, None),
        P("seg", "op"),
        P(),
        P("seg", None),
        P("seg", None),
    )
    return jax.shard_map(
        per_device,
        mesh=mesh,
        in_specs=placed,
        out_specs=(P("seg", "op", None), P("seg"), P("seg", "op", None, None)),
        check_vma=False,
    )
```

time: 470 us -> 80.8 us (0.17); the launches traced: 461 us -> 80.3 us
  waiting for transfers between devices: 358 us -> 0 us
  Pallas kernels: 0 us -> 72.5 us
  matrix products: 57.4 us -> 0 us
  other arithmetic: 18.9 us -> 0 us
  between operations: 17.9 us -> 3.04 us
    psum x2 -> x0, waiting for transfers between devices: 276 us -> none  [full_apply(): return lax.psum(partial_value, 'op')]
    all_gather x1 -> x0, waiting for transfers between devices: 80.5 us -> none  [per_device(): gathered = lax.all_gather(wavefunction, 'op', axis=1, tiled=True)[0]]
    pallas_call x0 -> x1, Pallas kernels: none -> 72.5 us  [per_device(): pl.pallas_call(kernel, name='segment_step', out_shape=(jax.ShapeDtypeStru...]
    dot_general x6 -> x0, matrix products: 57.4 us -> none  [the longest x2 25.8 us: local_terms(): partial_value = jnp.einsum('kab,bc->kac', left_ops, vector, precision=HIGH)]
    reduce_sum x3 -> x0, other arithmetic: 9.04 us -> none  [the longest x1 4.82 us: per_device(): energy = jnp.sum(initial * image_one) / width]
    broadcast_in_dim x2 -> x0, other arithmetic: 5.67 us -> none  [per_device(): return (chebyshev[None], jnp.reshape(energy, (1,)), handed[None])]
  transfers between devices with their start and end apart: 4 -> 0, of which waited for: 3 -> 0; matrix products, arithmetic and copies ran while one was open for 12% -> 0% of each run, Pallas kernels for 0% -> 0%
where the time goes in v1:
time: 80.8 us; the launch traced here: 80.3 us
  Pallas kernels  72.5 us (90%)
  local copies, waits for them, and re-layouts  4.74 us (6%)
  between operations  3.04 us (4%)
    pallas_call x1, Pallas kernels, per_device(): pl.pallas_call(kernel, name='segment_step', out_shape=(jax.ShapeDtypeStru...  72.5 us
    unnamed x2, local copies, waits for them, and re-layouts  4.74 us

profile of v1, /device:TPU:8, one launch (start us, length us, event | category | flops | bytes accessed | tf_op | source)
XLA Modules:
  0.0 80.3 jit_solution(1977681869752968687)
XLA Ops:
  1.3 72.5 %segment_step.1 = (f32[24,768]{1,0:T(8,128)}, f32[1]{0:T(128)}, f32[768,768]{1,0:T(8,128)}) custom-call(f32[768,768]{1,0:T(8,128)} %bitcast.6, f32[768,768]{1,0:T(8,128)} %bitcast.7, f32[768,768]{1,0:T(8,128)} %bitcast.8, f32[24,768]{1,0:T(8,128)} %bitcast.10, s32[1,768]{1,0:T(1,128)} %left_charge_ref.1, s32[1,768]{1,0:T(1,128)} %right_charge_ref.1, ...), custom_call_target="tpu_custom_call" | custom-call | tf_op jit(solution)/shard_map/segment_step/pallas_call | solution.py:381
  73.8 1.5 %copy.15 = f32[1,24,768]{2,1,0:T(8,128)} copy(f32[1,24,768]{2,1,0:T(8,128)} %bitcast.11) | data formatting | bytes 147456
  75.9 3.2 %copy.17 = f32[1,1,768,768]{3,2,1,0:T(8,128)} copy(f32[1,1,768,768]{3,2,1,0:T(8,128)} %bitcast.9) | data formatting | bytes 4718592

commit v2 on v1

v2 whole, which is shorter than its diff:
```python
import functools
import jax
import jax.numpy as jnp
from jax import lax
from jax.experimental import pallas as pl
from jax.experimental.pallas import tpu as pltpu
from jax.sharding import PartitionSpec as P

MESH = pl.DeviceIdType.MESH
F32, BF16 = jnp.float32, jnp.bfloat16
NX, NZ = 4, 8
SECTORS = 3
M = 768
Q = M // SECTORS
ROWS = 8
OPS = NX * NZ
OWN = SECTORS * ROWS
X_FAR = (2, 1, 3)
Z_FAR = (4, 3, 5, 2, 6, 1, 7)
DIRECT = [(dx, dz) for dz in Z_FAR + (0,) for dx in X_FAR + (0,) if (dx, dz) != (0, 0)]
Z_GROUPS = ((4,), (3, 5), (2, 6), (1, 7), (0,))
Z_GROUP = {d: i for i, group in enumerate(Z_GROUPS) for d in group}
ARRIVALS = (("x", (1, 3)), ("z", (1, 7)), ("x", (2,)), ("z", (2, 6)), ("z", (3, 5)), ("z", (4,)))
COPIES = 6
NN = (((1,), (0,)), ((), ()))
NT = (((1,), (1,)), ((), ()))


def dot(a, b, dims=NN):
    return lax.dot_general(a, b, dims, preferred_element_type=F32)


def dot3(a_high, a_low, b_high, b_low):
    return dot(a_high, b_high) + (dot(a_high, b_low) + dot(a_low, b_high))


def halves(value):
    high = value.astype(BF16)
    low = (value - high.astype(F32)).astype(BF16)
    return high, low


def thirds(value):
    high = value.astype(BF16)
    rest = value - high.astype(F32)
    middle = rest.astype(BF16)
    low = (rest - middle.astype(F32)).astype(BF16)
    return high, middle, low


def peer(dx, dz):
    op = lax.axis_index("op")
    x, z = op // NZ, op % NZ
    return lax.rem(x + dx, NX) * NZ + lax.rem(z + dz, NZ)


def third_dot(value, other, dims):
    rows = value.shape[0]
    stacked = dot(jnp.concatenate(thirds(value), 0), other, dims)
    return stacked[:rows] + stacked[rows : 2 * rows] + stacked[2 * rows :]


def kernel(
    left_hbm, right_hbm, basis_hbm, wave_ref, left_charge_ref, right_charge_ref, term_ref, coupling_ref,
    cheb_ref, energy_ref, handed_hbm,
    left, right, basis, load_sem,
    left_high, left_low, right_high, right_low,
    basis_high, basis_low, turned_high, turned_low, half_high, half_low, rotated,
    to_left, to_right, from_left, position_column,
    scratch_high, scratch_low, y_high, y_low, x_high, x_low,
    initial, first, gather_one, gather_two, partial_one, partial_two,
    land_one, land_two, send_sems, recv_sems, hand_send, hand_recv,
):
    seg, op = lax.axis_index("seg"), lax.axis_index("op")
    x, z = op // NZ, op % NZ
    width = float(M * M)
    segs = lax.axis_size("seg")

    loads = [
        pltpu.make_async_copy(source, target, load_sem.at[i])
        for i, (source, target) in enumerate(((right_hbm, right), (left_hbm, left), (basis_hbm, basis)))
    ]
    for load in loads:
        load.start()
    barrier = pltpu.get_barrier_semaphore()
    for dx, dz in DIRECT:
        pl.semaphore_signal(barrier, inc=1, device_id={"op": peer(dx, dz)}, device_id_type=MESH)
    for ds in (1, segs - 1):
        pl.semaphore_signal(barrier, inc=1, device_id={"seg": lax.rem(seg + ds, segs)}, device_id_type=MESH)

    before = lax.broadcasted_iota(jnp.int32, (M, M), 0) < lax.broadcasted_iota(jnp.int32, (M, M), 1)
    to_left[...] = jnp.where(before, 1.0, 0.0).astype(BF16)
    sector = lax.broadcasted_iota(jnp.int32, (8, M), 0)
    left_hits = jnp.where(left_charge_ref[...] == sector, 1.0, 0.0)
    right_hits = jnp.where(right_charge_ref[...] == sector, 1.0, 0.0)
    counts = dot(jnp.concatenate([left_hits, right_hits], 0).astype(BF16), to_left[...])
    left_rank = jnp.sum(left_hits * counts[:8], 0, keepdims=True)
    right_rank = jnp.sum(right_hits * counts[8:], 0, keepdims=True)
    left_place = left_charge_ref[...] * Q + left_rank.astype(jnp.int32)
    right_place = right_charge_ref[...] * Q + right_rank.astype(jnp.int32)
    place = lax.broadcasted_iota(jnp.int32, (M, M), 0)
    to_right[...] = jnp.where(place == right_place, 1.0, 0.0).astype(BF16)
    position_column[...] = jnp.transpose(jnp.broadcast_to(left_place.astype(F32), (128, M)))

    own_position = position_column[pl.ds(pl.multiple_of(op * OWN, 8), OWN), 0:1]
    moved = third_dot(wave_ref[...], to_right[...], NT)
    own_rows = jnp.where(
        own_position < Q, moved[:, :Q], jnp.where(own_position < 2 * Q, moved[:, Q : 2 * Q], moved[:, 2 * Q :])
    )
    for p in range(SECTORS):
        gather_one[p, x, z] = own_rows[p * ROWS : (p + 1) * ROWS]

    pl.semaphore_wait(barrier, len(DIRECT) + 2)

    def copy_of(source, target, sends, recvs, send_at, recv_at, dx=0, dz=1):
        return pltpu.make_async_remote_copy(
            source, target, sends.at[send_at], recvs.at[recv_at],
            device_id={"op": peer(dx, dz)}, device_id_type=MESH,
        )

    def gather(buffer, sends, recvs):
        def send(ref, send_at, recv_at, dx, dz):
            copy_of(ref, ref, sends, recvs, send_at, recv_at, dx, dz).start()

        def whole(send_at, recv_at):
            view = (
                buffer.at[0, 0:3, 0], buffer.at[1:3, 0, 0:7], buffer.at[0, :, 0:7], buffer.at[1:3, 0:3],
            )[send_at]
            return copy_of(view, view, sends, recvs, send_at, recv_at)

        def pass_a(away):
            ref = buffer.at[0, lax.rem(x - away + NX, NX), z]
            for d in Z_FAR:
                send(ref, 2, 6, 0, d)

        def pass_b(away):
            ref = buffer.at[1:3, x, lax.rem(z - away + NZ, NZ)]
            for d in X_FAR:
                send(ref, 3, 7, d, 0)

        def start_a():
            ref = buffer.at[0, x, z]
            for d in X_FAR:
                send(ref, 0, 0 if d == 2 else 1, d, 0)
            pass_a(0)

        def start_b():
            ref = buffer.at[1:3, x, z]
            for d in Z_FAR:
                send(ref, 1, 2 + Z_GROUP[d], 0, d)
            pass_b(0)

        def turn():
            for axis, group in ARRIVALS:
                if axis == "x":
                    view = buffer.at[0, 0 : len(group), 0]
                    copy_of(view, view, sends, recvs, 0, 0 if group == (2,) else 1).wait_recv()
                    for away in group:
                        pass_a(away)
                else:
                    view = buffer.at[1:3, 0, 0 : len(group)]
                    copy_of(view, view, sends, recvs, 1, 2 + Z_GROUP[group[0]]).wait_recv()
                    for away in group:
                        pass_b(away)

        def finish():
            whole(2, 6).wait_recv()
            whole(3, 7).wait_recv()

        def drain():
            for at in range(4):
                whole(at, 0).wait_send()

        return start_a, start_b, turn, finish, drain

    def scatter(partial, land, sends, recvs):
        land_a, land_x, middle, land_z = land

        def start_a():
            for dx, dz in DIRECT:
                ref = partial.at[0, lax.rem(x + dx, NX), lax.rem(z + dz, NZ)]
                copy_of(ref, land_a.at[dx * NZ + dz], sends, recvs, 0, 0, dx, dz).start()

        def start_b(p):
            for dz in Z_FAR + (0,):
                for dx in X_FAR:
                    ref = partial.at[p, lax.rem(x + dx, NX), lax.rem(z + dz, NZ)]
                    copy_of(ref, land_x.at[dz, p - 1, dx - 1], sends, recvs, 1, 2 + Z_GROUP[dz], dx, 0).start()

        def turn():
            for group in Z_GROUPS:
                view = land_x.at[0 : len(group)]
                copy_of(view, view, sends, recvs, 1, 2 + Z_GROUP[group[0]]).wait_recv()
                for dz in group:
                    zt = lax.rem(z + dz, NZ)
                    middle[dz] = partial[1:3, x, zt] + (land_x[dz, :, 0] + land_x[dz, :, 1] + land_x[dz, :, 2])
                    if dz:
                        copy_of(middle.at[dz], land_z.at[dz], sends, recvs, 2, 1, 0, dz).start()

        def whole_a():
            return copy_of(land_a.at[1:OPS], land_a.at[1:OPS], sends, recvs, 0, 0)

        def whole_z():
            return copy_of(land_z.at[1:NZ], land_z.at[1:NZ], sends, recvs, 2, 1)

        def finish_a():
            whole_a().wait_recv()
            return partial[0, x, z] + sum(land_a[dx * NZ + dz] for dx, dz in DIRECT)

        def finish_b():
            whole_z().wait_recv()
            return middle[0] + sum(land_z[dz] for dz in Z_FAR)

        def drain():
            whole_a().wait_send()
            copy_of(land_x, land_x, sends, recvs, 1, 0).wait_send()
            whole_z().wait_send()

        return start_a, start_b, turn, finish_a, finish_b, drain

    def blocks(body):
        @pl.loop(0, SECTORS)
        def _(i):
            body(pl.ds(pl.multiple_of(i * Q, Q), Q))

    def sort_columns(source, order):
        def body(rows):
            part_high, part_low = halves(source[rows, :])
            scratch_high[rows, :] = dot(part_high, order[...], NT).astype(BF16)
            scratch_low[rows, :] = dot(part_low, order[...], NT).astype(BF16)

        blocks(body)

    def sort_rows(order, source, target):
        def body(rows):
            target[rows, :] = dot(order[rows, :], source[...]).astype(BF16)

        blocks(body)

    def split_basis():
        def body(rows):
            basis_high[rows, :], basis_low[rows, :] = halves(basis[rows, :])

        blocks(body)
        for i in range(M // 128):
            cols = pl.ds(i * 128, 128)
            turned_high[:, cols], turned_low[:, cols] = halves(jnp.transpose(basis[cols, :]))

    def first_turn():
        def body(rows):
            part_high, part_low = halves(left[rows, :])
            value = dot3(part_high, part_low, basis_high[...], basis_low[...])
            half_high[rows, :], half_low[rows, :] = halves(value)

        blocks(body)

    def second_turn():
        for i in range(SECTORS):
            rows = pl.ds(i * Q, Q)
            rotated[rows, :] = dot3(turned_high[rows, :], turned_low[rows, :], half_high[...], half_low[...])

            @pl.when(seg < segs - 1)
            def _():
                hand(i).start()

    def hand(i):
        rows = pl.ds(i * Q, Q)
        return pltpu.make_async_remote_copy(
            rotated.at[rows, :], handed_hbm.at[rows, :], hand_send.at[i], hand_recv.at[i],
            device_id={"seg": lax.rem(seg + 1, segs)}, device_id_type=MESH,
        )

    coefficient = coupling_ref[term_ref[0, 0]]

    def inner(p):
        rows = pl.ds(p * Q, Q)
        value = coefficient * dot3(left_high[:, rows], left_low[:, rows], x_high[rows, :], x_low[rows, :])
        y_high[:, rows], y_low[:, rows] = halves(value)

    def outer(p):
        rows = pl.ds(p * Q, Q)
        return dot3(y_high[rows, :], y_low[rows, :], right_high[:, rows], right_low[:, rows])

    start_a, start_b, turn, finish, drain_one = gather(gather_one, send_sems[0], recv_sems[0])
    start_b()
    start_a()
    to_left[...] = jnp.where(place == left_place, 1.0, 0.0).astype(BF16)
    loads[0].wait()
    sort_columns(right, to_right)
    sort_rows(to_right, scratch_high, right_high)
    turn()
    sort_rows(to_right, scratch_low, right_low)
    loads[1].wait()
    sort_columns(left, to_left)
    sort_rows(to_left, scratch_high, left_high)
    sort_rows(to_left, scratch_low, left_low)
    finish()

    whole = gather_one[...].reshape(SECTORS, OPS, ROWS, Q)
    masked = jnp.stack([whole[p] for p in range(SECTORS)], 1).reshape(M, Q)
    scale = jnp.sqrt(jnp.sum(masked * masked) / width + 1e-06)
    masked_high, masked_low = halves(masked / scale)
    sorted_high = dot(to_left[...], masked_high)
    sorted_low = dot(to_left[...], masked_low)
    x_high[...] = sorted_high.astype(BF16)
    x_low[...] = sorted_low.astype(BF16)
    initial[...] = sorted_high + sorted_low
    own_initial = own_rows / scale

    for p in range(SECTORS):
        inner(p)
    start_a, start_b, turn, finish_a, finish_b, drain_two = scatter(
        partial_one, land_one, send_sems[1], recv_sems[1]
    )
    for p in (1, 2, 0):
        partial_one[p] = outer(p).reshape(NX, NZ, ROWS, Q)
        if p:
            start_b(p)
        else:
            start_a()

    loads[2].wait()
    split_basis()
    first_turn()
    turn()
    second_turn()
    gather_a, gather_b, turn, finish, drain_three = gather(gather_two, send_sems[2], recv_sems[2])
    gather_two[0, x, z] = finish_a()
    gather_a()
    gather_two[1:3, x, z] = finish_b()
    gather_b()

    lane = lax.broadcasted_iota(jnp.int32, (M, 128), 1).astype(F32)
    for i in range(M // 128):
        hits = position_column[...] == lane + float(i * 128)
        from_left[:, i * 128 : (i + 1) * 128] = jnp.where(hits, 1.0, 0.0).astype(BF16)
    turn()
    finish()

    image = gather_two[...].reshape(M, Q)
    start = initial[...]
    energy = jnp.sum(start * image) / width
    spread = jnp.sqrt(jnp.sum(image * image) / width + 1e-06)
    energy_ref[0] = energy
    step = (image - energy * start) / spread
    first[...] = step
    x_high[...], x_low[...] = halves(step)
    for p in range(SECTORS):
        inner(p)
    for p in range(SECTORS):
        out_high, out_low = halves(outer(p))
        rows = pl.ds(p * Q, Q)
        y_high[rows, 0:Q] = out_high
        y_low[rows, 0:Q] = out_low
    back = dot(from_left[...], y_high[:, 0:Q]) + dot(from_left[...], y_low[:, 0:Q])
    back = back.reshape(OPS, SECTORS, ROWS, Q)
    start_a, start_b, turn, finish_a, finish_b, drain_four = scatter(
        partial_two, land_two, send_sems[3], recv_sems[3]
    )
    for p in (1, 2, 0):
        partial_two[p] = back[:, p].reshape(NX, NZ, ROWS, Q)
        if p:
            start_b(p)
        else:
            start_a()

    own_select = jnp.where(
        own_position == lax.broadcasted_iota(jnp.int32, (OWN, M), 1).astype(F32), 1.0, 0.0
    ).astype(BF16)
    own_step = sum(dot(own_select, part) for part in thirds(first[...]))
    turn()
    own_image = jnp.concatenate([finish_a(), finish_b().reshape(2 * ROWS, Q)], 0)
    result = 2.0 * (own_image - energy * own_step) / spread - own_initial
    spread_out = jnp.concatenate(
        [
            jnp.where((own_position >= p * Q) & (own_position < (p + 1) * Q), result, 0.0)
            for p in range(SECTORS)
        ],
        1,
    )
    cheb_ref[...] = third_dot(spread_out, to_right[...], NN)

    for drain in (drain_one, drain_two, drain_three, drain_four):
        drain()

    @pl.when(seg < segs - 1)
    def _():
        for i in range(SECTORS):
            hand(i).wait_send()

    @pl.when(seg > 0)
    def _():
        for i in range(SECTORS):
            hand(i).wait_recv()


def place_results(cheb_raw, energy_raw, handed_raw, left_hbm, cheb_ref, energy_ref, handed_hbm, held, in_sems, out_sems):
    energy_ref[0] = energy_raw[0]
    cheb_ref[...] = cheb_raw[...]
    rows = M // COPIES

    def fetch(source, i):
        part = pl.ds(i * rows, rows)
        return pltpu.make_async_copy(source.at[part, :], held.at[part, :], in_sems.at[i])

    def put(i):
        part = pl.ds(i * rows, rows)
        return pltpu.make_async_copy(held.at[part, :], handed_hbm.at[part, :], out_sems.at[i])

    @pl.when(lax.axis_index("seg") == 0)
    def _():
        for i in range(COPIES):
            fetch(left_hbm, i).start()

    @pl.when(lax.axis_index("seg") > 0)
    def _():
        for i in range(COPIES):
            fetch(handed_raw, i).start()

    for i in range(COPIES):
        fetch(handed_raw, i).wait()
        put(i).start()
    for i in range(COPIES):
        put(i).wait()


def per_device(
    left_ops,
    right_ops,
    wavefunction,
    basis_rotation,
    pair_term,
    coupling,
    left_charge,
    right_charge,
):
    vmem, smem, hbm = (
        pl.BlockSpec(memory_space=space) for space in (pltpu.VMEM, pltpu.SMEM, pl.ANY)
    )
    dma = pltpu.SemaphoreType.DMA

    def full(dtype):
        return pltpu.VMEM((M, M), dtype)

    def parts():
        return pltpu.VMEM((SECTORS, NX, NZ, ROWS, Q), F32)

    def tall(dtype):
        return pltpu.VMEM((M, Q), dtype)

    land = [
        pltpu.VMEM((OPS, ROWS, Q), F32), pltpu.VMEM((NZ, 2, NX - 1, ROWS, Q), F32),
        pltpu.VMEM((NZ, 2, ROWS, Q), F32), pltpu.VMEM((NZ, 2, ROWS, Q), F32),
    ]
    results = (
        jax.ShapeDtypeStruct((OWN, M), F32),
        jax.ShapeDtypeStruct((1,), F32),
        jax.ShapeDtypeStruct((M, M), F32),
    )
    own_left = left_ops[0, 0]
    cheb, energy, handed = pl.pallas_call(
        kernel,
        name="segment_step",
        out_shape=results,
        in_specs=[hbm, hbm, hbm, vmem, vmem, vmem, smem, smem],
        out_specs=(vmem, smem, hbm),
        scratch_shapes=[
            full(F32), full(F32), full(F32), dma((3,)),
            full(BF16), full(BF16), full(BF16), full(BF16),
            full(BF16), full(BF16), full(BF16), full(BF16), full(BF16), full(BF16), full(F32),
            full(BF16), full(BF16), full(BF16), pltpu.VMEM((M, 128), F32),
            full(BF16), full(BF16), full(BF16), full(BF16), tall(BF16), tall(BF16),
            tall(F32), tall(F32), parts(), parts(), parts(), parts(),
            list(land), list(land),
            [dma((4,)), dma((3,)), dma((4,)), dma((3,))], [dma((8,)), dma((7,)), dma((8,)), dma((7,))], dma((SECTORS,)), dma((SECTORS,)),
        ],
        compiler_params=pltpu.CompilerParams(
            collective_id=0, has_side_effects=True, vmem_limit_bytes=58 * 2**20
        ),
    )(
        own_left, right_ops[0, 0], basis_rotation[0], wavefunction[0],
        left_charge, right_charge, pair_term, coupling,
    )
    cheb, energy, handed = pl.pallas_call(
        place_results,
        name="place_results",
        out_shape=results,
        in_specs=[vmem, smem, hbm, hbm],
        out_specs=(vmem, smem, hbm),
        scratch_shapes=[full(F32), dma((COPIES,)), dma((COPIES,))],
    )(cheb, energy, handed, own_left)
    return cheb[None], energy, handed[None, None]


def solution(mesh):
    placed = (
        P("seg", "op", None, None),
        P("seg", "op", None, None),
        P("seg", "op", None),
        P("seg", None, None),
        P("seg", "op"),
        P(),
        P("seg", None),
        P("seg", None),
    )
    return jax.shard_map(
        per_device,
        mesh=mesh,
        in_specs=placed,
        out_specs=(P("seg", "op", None), P("seg"), P("seg", "op", None, None)),
        check_vma=False,
    )
```

time: 80.8 us -> 73.8 us (0.913)
  local copies, waits for them, and re-layouts: 4.74 us -> 0 us
  between operations: 3.04 us -> 1.45 us
    unnamed x2 -> x0, local copies, waits for them, and re-layouts: 4.74 us -> none
    pallas_call x1 -> x2, Pallas kernels: 72.5 us -> 71.8 us  [the longest x1 67.1 us: per_device(): pl.pallas_call(kernel, name='segment_step', out_shape=results, in_specs=[...]
where the time goes in v2:
time: 73.8 us; the launch traced here: 73.2 us
  Pallas kernels  71.8 us (97%)
  between operations  1.45 us (2%)
    pallas_call x1, Pallas kernels, per_device(): pl.pallas_call(kernel, name='segment_step', out_shape=results, in_specs=[...  67.1 us
    pallas_call x1, Pallas kernels, per_device(): pl.pallas_call(place_results, name='place_results', out_shape=results, in...  4.64 us

profile of v2, /device:TPU:8, one launch (start us, length us, event | category | flops | bytes accessed | tf_op | source)
XLA Modules:
  0.0 73.2 jit_solution(12115919420371185018)
XLA Ops:
  1.3 67.1 %segment_step.1 = (f32[24,768]{1,0:T(8,128)}, f32[1]{0:T(128)}, f32[768,768]{1,0:T(8,128)}) custom-call(f32[768,768]{1,0:T(8,128)} %bitcast.6, f32[768,768]{1,0:T(8,128)} %bitcast.8, f32[768,768]{1,0:T(8,128)} %bitcast.9, f32[24,768]{1,0:T(8,128)} %bitcast.10, s32[1,768]{1,0:T(1,128)} %left_charge_ref.1, s32[1,768]{1,0:T(1,128)} %right_charge_ref.1, ...), custom_call_target="tpu_custom_call" | custom-call | tf_op jit(solution)/shard_map/segment_step/pallas_call | solution.py:461
  68.4 4.6 %place_results.1 = (f32[24,768]{1,0:T(8,128)}, f32[1]{0:T(128)}, f32[768,768]{1,0:T(8,128)}) custom-call(f32[24,768]{1,0:T(8,128)} %get-tuple-element.9.cheb_raw, f32[1]{0:T(128)} %get-tuple-element.10.energy_raw, f32[768,768]{1,0:T(8,128)} %get-tuple-element.11.handed_raw, f32[768,768]{1,0:T(8,128)} %bitcast.7), custom_call_target="tpu_custom_call" | custom-call | tf_op jit(solution)/shard_map/place_results/pallas_call | solution.py:484

commit v3 on v2

--- a/solution.py
+++ b/solution.py
@@ -13,6 +13,8 @@
 M = 768
 Q = M // SECTORS
 ROWS = 8
+HALF = 128
+PARTS = 2 * SECTORS
 OPS = NX * NZ
 OWN = SECTORS * ROWS
 X_FAR = (2, 1, 3)
@@ -20,8 +22,8 @@
 DIRECT = [(dx, dz) for dz in Z_FAR + (0,) for dx in X_FAR + (0,) if (dx, dz) != (0, 0)]
 Z_GROUPS = ((4,), (3, 5), (2, 6), (1, 7), (0,))
 Z_GROUP = {d: i for i, group in enumerate(Z_GROUPS) for d in group}
+CROSS = [(dx, 0) for dx in X_FAR] + [(0, dz) for dz in Z_FAR]
 ARRIVALS = (("x", (1, 3)), ("z", (1, 7)), ("x", (2,)), ("z", (2, 6)), ("z", (3, 5)), ("z", (4,)))
-COPIES = 6
 NN = (((1,), (0,)), ((), ()))
 NT = (((1,), (1,)), ((), ()))
 
@@ -61,9 +63,9 @@
 
 
 def kernel(
-    left_hbm, right_hbm, basis_hbm, wave_ref, left_charge_ref, right_charge_ref, term_ref, coupling_ref,
-    cheb_ref, energy_ref, handed_hbm,
-    left, right, basis, load_sem,
+    left_hbm, right_hbm, basis_hbm, wave_hbm, left_charge_hbm, right_charge_hbm, term_hbm, coupling_hbm,
+    cheb_ref, energy_ref, handed_ref,
+    left, right, basis, wave_ref, left_charge_ref, right_charge_ref, term_ref, coupling_ref, load_sem,
     left_high, left_low, right_high, right_low,
     basis_high, basis_low, turned_high, turned_low, half_high, half_low, rotated,
     to_left, to_right, from_left, position_column,
@@ -78,19 +80,35 @@
 
     loads = [
         pltpu.make_async_copy(source, target, load_sem.at[i])
-        for i, (source, target) in enumerate(((right_hbm, right), (left_hbm, left), (basis_hbm, basis)))
+        for i, (source, target) in enumerate(
+            (
+                (right_charge_hbm, right_charge_ref), (left_charge_hbm, left_charge_ref), (wave_hbm, wave_ref),
+                (right_hbm, right), (left_hbm, left), (basis_hbm, basis),
+                (term_hbm, term_ref), (coupling_hbm, coupling_ref),
+            )
+        )
     ]
-    for load in loads:
+    for load in loads[:3]:
         load.start()
     barrier = pltpu.get_barrier_semaphore()
-    for dx, dz in DIRECT:
+    for dx, dz in CROSS:
         pl.semaphore_signal(barrier, inc=1, device_id={"op": peer(dx, dz)}, device_id_type=MESH)
     for ds in (1, segs - 1):
         pl.semaphore_signal(barrier, inc=1, device_id={"seg": lax.rem(seg + ds, segs)}, device_id_type=MESH)
 
+    for load in loads[3:]:
+        load.start()
+    kept = pltpu.make_async_copy(left_hbm, handed_ref, load_sem.at[8])
+
+    @pl.when(seg == 0)
+    def _():
+        kept.start()
+
     before = lax.broadcasted_iota(jnp.int32, (M, M), 0) < lax.broadcasted_iota(jnp.int32, (M, M), 1)
     to_left[...] = jnp.where(before, 1.0, 0.0).astype(BF16)
     sector = lax.broadcasted_iota(jnp.int32, (8, M), 0)
+    loads[0].wait()
+    loads[1].wait()
     left_hits = jnp.where(left_charge_ref[...] == sector, 1.0, 0.0)
     right_hits = jnp.where(right_charge_ref[...] == sector, 1.0, 0.0)
     counts = dot(jnp.concatenate([left_hits, right_hits], 0).astype(BF16), to_left[...])
@@ -103,14 +121,16 @@
     position_column[...] = jnp.transpose(jnp.broadcast_to(left_place.astype(F32), (128, M)))
 
     own_position = position_column[pl.ds(pl.multiple_of(op * OWN, 8), OWN), 0:1]
+    loads[2].wait()
     moved = third_dot(wave_ref[...], to_right[...], NT)
     own_rows = jnp.where(
         own_position < Q, moved[:, :Q], jnp.where(own_position < 2 * Q, moved[:, Q : 2 * Q], moved[:, 2 * Q :])
     )
-    for p in range(SECTORS):
-        gather_one[p, x, z] = own_rows[p * ROWS : (p + 1) * ROWS]
-
-    pl.semaphore_wait(barrier, len(DIRECT) + 2)
+    for c in range(PARTS):
+        p, cols = c // 2, slice(c % 2 * HALF, (c % 2 + 1) * HALF)
+        gather_one[c, x, z] = own_rows[p * ROWS : (p + 1) * ROWS, cols]
+
+    pl.semaphore_wait(barrier, len(CROSS) + 2)
 
     def copy_of(source, target, sends, recvs, send_at, recv_at, dx=0, dz=1):
         return pltpu.make_async_remote_copy(
@@ -124,7 +144,7 @@
 
         def whole(send_at, recv_at):
             view = (
-                buffer.at[0, 0:3, 0], buffer.at[1:3, 0, 0:7], buffer.at[0, :, 0:7], buffer.at[1:3, 0:3],
+                buffer.at[0, 0:3, 0], buffer.at[1:PARTS, 0, 0:7], buffer.at[0, :, 0:7], buffer.at[1:PARTS, 0:3],
             )[send_at]
             return copy_of(view, view, sends, recvs, send_at, recv_at)
 
@@ -134,7 +154,7 @@
                 send(ref, 2, 6, 0, d)
 
         def pass_b(away):
-            ref = buffer.at[1:3, x, lax.rem(z - away + NZ, NZ)]
+            ref = buffer.at[1:PARTS, x, lax.rem(z - away + NZ, NZ)]
             for d in X_FAR:
                 send(ref, 3, 7, d, 0)
 
@@ -145,20 +165,20 @@
             pass_a(0)
 
         def start_b():
-            ref = buffer.at[1:3, x, z]
+            ref = buffer.at[1:PARTS, x, z]
             for d in Z_FAR:
                 send(ref, 1, 2 + Z_GROUP[d], 0, d)
             pass_b(0)
 
-        def turn():
-            for axis, group in ARRIVALS:
+        def turn(arrivals):
+            for axis, group in arrivals:
                 if axis == "x":
                     view = buffer.at[0, 0 : len(group), 0]
                     copy_of(view, view, sends, recvs, 0, 0 if group == (2,) else 1).wait_recv()
                     for away in group:
                         pass_a(away)
                 else:
-                    view = buffer.at[1:3, 0, 0 : len(group)]
+                    view = buffer.at[1:PARTS, 0, 0 : len(group)]
                     copy_of(view, view, sends, recvs, 1, 2 + Z_GROUP[group[0]]).wait_recv()
                     for away in group:
                         pass_b(away)
@@ -181,19 +201,19 @@
                 ref = partial.at[0, lax.rem(x + dx, NX), lax.rem(z + dz, NZ)]
                 copy_of(ref, land_a.at[dx * NZ + dz], sends, recvs, 0, 0, dx, dz).start()
 
-        def start_b(p):
+        def start_b():
             for dz in Z_FAR + (0,):
                 for dx in X_FAR:
-                    ref = partial.at[p, lax.rem(x + dx, NX), lax.rem(z + dz, NZ)]
-                    copy_of(ref, land_x.at[dz, p - 1, dx - 1], sends, recvs, 1, 2 + Z_GROUP[dz], dx, 0).start()
-
-        def turn():
-            for group in Z_GROUPS:
+                    ref = partial.at[1:PARTS, lax.rem(x + dx, NX), lax.rem(z + dz, NZ)]
+                    copy_of(ref, land_x.at[dz, dx - 1], sends, recvs, 1, 2 + Z_GROUP[dz], dx, 0).start()
+
+        def turn(groups):
+            for group in groups:
                 view = land_x.at[0 : len(group)]
                 copy_of(view, view, sends, recvs, 1, 2 + Z_GROUP[group[0]]).wait_recv()
                 for dz in group:
-                    zt = lax.rem(z + dz, NZ)
-                    middle[dz] = partial[1:3, x, zt] + (land_x[dz, :, 0] + land_x[dz, :, 1] + land_x[dz, :, 2])
+                    own = partial[1:PARTS, x, lax.rem(z + dz, NZ)]
+                    middle[dz] = own + (land_x[dz, 0] + land_x[dz, 1] + land_x[dz, 2])
                     if dz:
                         copy_of(middle.at[dz], land_z.at[dz], sends, recvs, 2, 1, 0, dz).start()
 
@@ -219,9 +239,8 @@
         return start_a, start_b, turn, finish_a, finish_b, drain
 
     def blocks(body):
-        @pl.loop(0, SECTORS)
-        def _(i):
-            body(pl.ds(pl.multiple_of(i * Q, Q), Q))
+        for i in range(SECTORS):
+            body(pl.ds(i * Q, Q))
 
     def sort_columns(source, order):
         def body(rows):
@@ -254,8 +273,8 @@
 
         blocks(body)
 
-    def second_turn():
-        for i in range(SECTORS):
+    def second_turn(steps):
+        for i in steps:
             rows = pl.ds(i * Q, Q)
             rotated[rows, :] = dot3(turned_high[rows, :], turned_low[rows, :], half_high[...], half_low[...])
 
@@ -266,11 +285,17 @@
     def hand(i):
         rows = pl.ds(i * Q, Q)
         return pltpu.make_async_remote_copy(
-            rotated.at[rows, :], handed_hbm.at[rows, :], hand_send.at[i], hand_recv.at[i],
+            rotated.at[rows, :], handed_ref.at[rows, :], hand_send.at[i], hand_recv.at[i],
             device_id={"seg": lax.rem(seg + 1, segs)}, device_id_type=MESH,
         )
 
-    coefficient = coupling_ref[term_ref[0, 0]]
+    def keep(partial, p, value):
+        partial[2 * p] = value[:, :HALF].reshape(NX, NZ, ROWS, HALF)
+        partial[2 * p + 1] = value[:, HALF:].reshape(NX, NZ, ROWS, HALF)
+
+    def blocks_of(buffer, p):
+        return jnp.concatenate([buffer[c].reshape(Q, HALF) for c in (2 * p, 2 * p + 1)], 1)
+
 
     def inner(p):
         rows = pl.ds(p * Q, Q)
@@ -285,19 +310,22 @@
     start_b()
     start_a()
     to_left[...] = jnp.where(place == left_place, 1.0, 0.0).astype(BF16)
-    loads[0].wait()
+    loads[3].wait()
     sort_columns(right, to_right)
     sort_rows(to_right, scratch_high, right_high)
-    turn()
+    turn(ARRIVALS[:2])
     sort_rows(to_right, scratch_low, right_low)
-    loads[1].wait()
+    turn(ARRIVALS[2:])
+    loads[4].wait()
     sort_columns(left, to_left)
     sort_rows(to_left, scratch_high, left_high)
     sort_rows(to_left, scratch_low, left_low)
     finish()
 
-    whole = gather_one[...].reshape(SECTORS, OPS, ROWS, Q)
-    masked = jnp.stack([whole[p] for p in range(SECTORS)], 1).reshape(M, Q)
+    loads[6].wait()
+    loads[7].wait()
+    coefficient = coupling_ref[term_ref[0, 0]]
+    masked = jnp.stack([blocks_of(gather_one, p).reshape(OPS, ROWS, Q) for p in range(SECTORS)], 1).reshape(M, Q)
     scale = jnp.sqrt(jnp.sum(masked * masked) / width + 1e-06)
     masked_high, masked_low = halves(masked / scale)
     sorted_high = dot(to_left[...], masked_high)
@@ -312,36 +340,40 @@
     start_a, start_b, turn, finish_a, finish_b, drain_two = scatter(
         partial_one, land_one, send_sems[1], recv_sems[1]
     )
-    for p in (1, 2, 0):
-        partial_one[p] = outer(p).reshape(NX, NZ, ROWS, Q)
-        if p:
-            start_b(p)
-        else:
-            start_a()
-
-    loads[2].wait()
+    for p in range(SECTORS):
+        keep(partial_one, p, outer(p))
+    start_b()
+    start_a()
+
+    loads[5].wait()
     split_basis()
     first_turn()
-    turn()
-    second_turn()
+    turn(Z_GROUPS[:2])
+    second_turn((0,))
+    turn(Z_GROUPS[2:4])
+    second_turn((1,))
+    turn(Z_GROUPS[4:])
     gather_a, gather_b, turn, finish, drain_three = gather(gather_two, send_sems[2], recv_sems[2])
     gather_two[0, x, z] = finish_a()
     gather_a()
-    gather_two[1:3, x, z] = finish_b()
+    second_turn((2,))
+    gather_two[1:PARTS, x, z] = finish_b()
     gather_b()
 
     lane = lax.broadcasted_iota(jnp.int32, (M, 128), 1).astype(F32)
+    by_part = position_column[...].reshape(OPS, SECTORS, ROWS, 128)
+    by_part = jnp.concatenate([by_part[:, p].reshape(Q, 128) for p in range(SECTORS)], 0)
     for i in range(M // 128):
-        hits = position_column[...] == lane + float(i * 128)
+        hits = by_part == lane + float(i * 128)
         from_left[:, i * 128 : (i + 1) * 128] = jnp.where(hits, 1.0, 0.0).astype(BF16)
-    turn()
+    turn(ARRIVALS)
     finish()
 
-    image = gather_two[...].reshape(M, Q)
+    image = jnp.concatenate([blocks_of(gather_two, p) for p in range(SECTORS)], 0)
     start = initial[...]
     energy = jnp.sum(start * image) / width
     spread = jnp.sqrt(jnp.sum(image * image) / width + 1e-06)
-    energy_ref[0] = energy
+    energy_ref[...] = jnp.full((8, 128), energy, F32)
     step = (image - energy * start) / spread
     first[...] = step
     x_high[...], x_low[...] = halves(step)
@@ -352,24 +384,26 @@
         rows = pl.ds(p * Q, Q)
         y_high[rows, 0:Q] = out_high
         y_low[rows, 0:Q] = out_low
-    back = dot(from_left[...], y_high[:, 0:Q]) + dot(from_left[...], y_low[:, 0:Q])
-    back = back.reshape(OPS, SECTORS, ROWS, Q)
     start_a, start_b, turn, finish_a, finish_b, drain_four = scatter(
         partial_two, land_two, send_sems[3], recv_sems[3]
     )
-    for p in (1, 2, 0):
-        partial_two[p] = back[:, p].reshape(NX, NZ, ROWS, Q)
-        if p:
-            start_b(p)
-        else:
-            start_a()
+    for p in range(SECTORS):
+        rows = pl.ds(p * Q, Q)
+        back = dot(from_left[rows, :], y_high[:, 0:Q]) + dot(from_left[rows, :], y_low[:, 0:Q])
+        keep(partial_two, p, back)
+    start_b()
+    start_a()
 
     own_select = jnp.where(
         own_position == lax.broadcasted_iota(jnp.int32, (OWN, M), 1).astype(F32), 1.0, 0.0
     ).astype(BF16)
     own_step = sum(dot(own_select, part) for part in thirds(first[...]))
-    turn()
-    own_image = jnp.concatenate([finish_a(), finish_b().reshape(2 * ROWS, Q)], 0)
+    turn(Z_GROUPS)
+    part, others = finish_a(), finish_b()
+    part = [part] + [others[c] for c in range(PARTS - 1)]
+    own_image = jnp.concatenate(
+        [jnp.concatenate(part[2 * p : 2 * p + 2], 1) for p in range(SECTORS)], 0
+    )
     result = 2.0 * (own_image - energy * own_step) / spread - own_initial
     spread_out = jnp.concatenate(
         [
@@ -393,35 +427,9 @@
         for i in range(SECTORS):
             hand(i).wait_recv()
 
-
-def place_results(cheb_raw, energy_raw, handed_raw, left_hbm, cheb_ref, energy_ref, handed_hbm, held, in_sems, out_sems):
-    energy_ref[0] = energy_raw[0]
-    cheb_ref[...] = cheb_raw[...]
-    rows = M // COPIES
-
-    def fetch(source, i):
-        part = pl.ds(i * rows, rows)
-        return pltpu.make_async_copy(source.at[part, :], held.at[part, :], in_sems.at[i])
-
-    def put(i):
-        part = pl.ds(i * rows, rows)
-        return pltpu.make_async_copy(held.at[part, :], handed_hbm.at[part, :], out_sems.at[i])
-
-    @pl.when(lax.axis_index("seg") == 0)
+    @pl.when(seg == 0)
     def _():
-        for i in range(COPIES):
-            fetch(left_hbm, i).start()
-
-    @pl.when(lax.axis_index("seg") > 0)
-    def _():
-        for i in range(COPIES):
-            fetch(handed_raw, i).start()
-
-    for i in range(COPIES):
-        fetch(handed_raw, i).wait()
-        put(i).start()
-    for i in range(COPIES):
-        put(i).wait()
+        kept.wait()
 
 
 def per_device(
@@ -434,38 +442,32 @@
     left_charge,
     right_charge,
 ):
-    vmem, smem, hbm = (
-        pl.BlockSpec(memory_space=space) for space in (pltpu.VMEM, pltpu.SMEM, pl.ANY)
-    )
+    vmem, hbm = (pl.BlockSpec(memory_space=space) for space in (pltpu.VMEM, pl.ANY))
     dma = pltpu.SemaphoreType.DMA
 
     def full(dtype):
         return pltpu.VMEM((M, M), dtype)
 
     def parts():
-        return pltpu.VMEM((SECTORS, NX, NZ, ROWS, Q), F32)
+        return pltpu.VMEM((PARTS, NX, NZ, ROWS, HALF), F32)
 
     def tall(dtype):
         return pltpu.VMEM((M, Q), dtype)
 
     land = [
-        pltpu.VMEM((OPS, ROWS, Q), F32), pltpu.VMEM((NZ, 2, NX - 1, ROWS, Q), F32),
-        pltpu.VMEM((NZ, 2, ROWS, Q), F32), pltpu.VMEM((NZ, 2, ROWS, Q), F32),
+        pltpu.VMEM((OPS, ROWS, HALF), F32), pltpu.VMEM((NZ, NX - 1, PARTS - 1, ROWS, HALF), F32),
+        pltpu.VMEM((NZ, PARTS - 1, ROWS, HALF), F32), pltpu.VMEM((NZ, PARTS - 1, ROWS, HALF), F32),
     ]
-    results = (
-        jax.ShapeDtypeStruct((OWN, M), F32),
-        jax.ShapeDtypeStruct((1,), F32),
-        jax.ShapeDtypeStruct((M, M), F32),
-    )
-    own_left = left_ops[0, 0]
     cheb, energy, handed = pl.pallas_call(
         kernel,
         name="segment_step",
-        out_shape=results,
-        in_specs=[hbm, hbm, hbm, vmem, vmem, vmem, smem, smem],
-        out_specs=(vmem, smem, hbm),
+        out_shape=(pltpu.VMEM((OWN, M), F32), pltpu.VMEM((8, 128), F32), pltpu.VMEM((M, M), F32)),
+        in_specs=[hbm] * 8,
+        out_specs=(vmem, vmem, vmem),
         scratch_shapes=[
-            full(F32), full(F32), full(F32), dma((3,)),
+            full(F32), full(F32), full(F32), pltpu.VMEM((OWN, M), F32),
+            pltpu.VMEM((1, M), jnp.int32), pltpu.VMEM((1, M), jnp.int32),
+            pltpu.SMEM((1, 1), jnp.int32), pltpu.SMEM((16,), F32), dma((9,)),
             full(BF16), full(BF16), full(BF16), full(BF16),
             full(BF16), full(BF16), full(BF16), full(BF16), full(BF16), full(BF16), full(F32),
             full(BF16), full(BF16), full(BF16), pltpu.VMEM((M, 128), F32),
@@ -475,21 +477,13 @@
             [dma((4,)), dma((3,)), dma((4,)), dma((3,))], [dma((8,)), dma((7,)), dma((8,)), dma((7,))], dma((SECTORS,)), dma((SECTORS,)),
         ],
         compiler_params=pltpu.CompilerParams(
-            collective_id=0, has_side_effects=True, vmem_limit_bytes=58 * 2**20
+            collective_id=0, has_side_effects=True, vmem_limit_bytes=57 * 2**20
         ),
     )(
-        own_left, right_ops[0, 0], basis_rotation[0], wavefunction[0],
+        left_ops[0, 0], right_ops[0, 0], basis_rotation[0], wavefunction[0],
         left_charge, right_charge, pair_term, coupling,
     )
-    cheb, energy, handed = pl.pallas_call(
-        place_results,
-        name="place_results",
-        out_shape=results,
-        in_specs=[vmem, smem, hbm, hbm],
-        out_specs=(vmem, smem, hbm),
-        scratch_shapes=[full(F32), dma((COPIES,)), dma((COPIES,))],
-    )(cheb, energy, handed, own_left)
-    return cheb[None], energy, handed[None, None]
+    return cheb[None], energy[0, :1], handed[None, None]
 
 
 def solution(mesh):

time: 73.8 us -> 67.9 us (0.920)
  Pallas kernels: 71.8 us -> 63.9 us
  local copies, waits for them, and re-layouts: 0 us -> 2.55 us
    pallas_call x2 -> x1, Pallas kernels: 71.8 us -> 63.9 us  [per_device(): pl.pallas_call(kernel, name='segment_step', out_shape=(pltpu.VMEM((OWN, M...]
    unnamed x0 -> x2, local copies, waits for them, and re-layouts: none -> 2.04 us
where the time goes in v3:
time: 67.9 us; the launch traced here: 67.7 us
  Pallas kernels  63.9 us (94%)
  local copies, waits for them, and re-layouts  2.55 us (4%)
  between operations  1.29 us (2%)
    pallas_call x1, Pallas kernels, per_device(): pl.pallas_call(kernel, name='segment_step', out_shape=(pltpu.VMEM((OWN, M...  63.9 us
    unnamed x2, local copies, waits for them, and re-layouts  2.04 us

profile of v3, /device:TPU:8, one launch (start us, length us, event | category | flops | bytes accessed | tf_op | source)
XLA Modules:
  0.0 67.7 jit_solution(13372930513150806579)
XLA Ops:
  1.3 63.9 %segment_step.1 = (f32[24,768]{1,0:T(8,128)S(1)}, f32[8,128]{1,0:T(8,128)S(1)}, f32[768,768]{1,0:T(8,128)S(1)}) custom-call(f32[768,768]{1,0:T(8,128)} %bitcast.9, f32[768,768]{1,0:T(8,128)} %bitcast.10, f32[768,768]{1,0:T(8,128)} %bitcast.11, f32[24,768]{1,0:T(8,128)} %bitcast.12, s32[1,768]{1,0:T(1,128)} %left_charge_hbm.1, s32[1,768]{1,0:T(1,128)} %right_charge_hbm.1, ...), custom_call_target="tpu_custom_call" | custom-call | tf_op jit(solution)/shard_map/segment_step/pallas_call | solution.py:461
  65.2 0.5 slice.3
  65.7 0.6 copy.13
  66.3 1.4 %copy.14 = f32[1,1,768,768]{3,2,1,0:T(8,128)} copy(f32[1,1,768,768]{3,2,1,0:T(8,128)S(1)} %bitcast.7) | data formatting | bytes 4718592

commit v4 on v3

--- a/solution.py
+++ b/solution.py
@@ -130,6 +130,23 @@
         p, cols = c // 2, slice(c % 2 * HALF, (c % 2 + 1) * HALF)
         gather_one[c, x, z] = own_rows[p * ROWS : (p + 1) * ROWS, cols]
 
+    def blocks(body):
+        for i in range(SECTORS):
+            body(pl.ds(i * Q, Q))
+
+    def sort_columns(source, order, which):
+        def body(rows):
+            part = halves(source[rows, :])[which]
+            (scratch_high, scratch_low)[which][rows, :] = dot(part, order[...], NT).astype(BF16)
+
+        blocks(body)
+
+    def sort_rows(order, source, target):
+        def body(rows):
+            target[rows, :] = dot(order[rows, :], source[...]).astype(BF16)
+
+        blocks(body)
+
     pl.semaphore_wait(barrier, len(CROSS) + 2)
 
     def copy_of(source, target, sends, recvs, send_at, recv_at, dx=0, dz=1):
@@ -238,24 +255,6 @@
 
         return start_a, start_b, turn, finish_a, finish_b, drain
 
-    def blocks(body):
-        for i in range(SECTORS):
-            body(pl.ds(i * Q, Q))
-
-    def sort_columns(source, order):
-        def body(rows):
-            part_high, part_low = halves(source[rows, :])
-            scratch_high[rows, :] = dot(part_high, order[...], NT).astype(BF16)
-            scratch_low[rows, :] = dot(part_low, order[...], NT).astype(BF16)
-
-        blocks(body)
-
-    def sort_rows(order, source, target):
-        def body(rows):
-            target[rows, :] = dot(order[rows, :], source[...]).astype(BF16)
-
-        blocks(body)
-
     def split_basis():
         def body(rows):
             basis_high[rows, :], basis_low[rows, :] = halves(basis[rows, :])
@@ -311,13 +310,15 @@
     start_a()
     to_left[...] = jnp.where(place == left_place, 1.0, 0.0).astype(BF16)
     loads[3].wait()
-    sort_columns(right, to_right)
+    sort_columns(right, to_right, 0)
+    sort_columns(right, to_right, 1)
     sort_rows(to_right, scratch_high, right_high)
     turn(ARRIVALS[:2])
     sort_rows(to_right, scratch_low, right_low)
     turn(ARRIVALS[2:])
     loads[4].wait()
-    sort_columns(left, to_left)
+    sort_columns(left, to_left, 0)
+    sort_columns(left, to_left, 1)
     sort_rows(to_left, scratch_high, left_high)
     sort_rows(to_left, scratch_low, left_low)
     finish()
@@ -356,9 +357,9 @@
     gather_a, gather_b, turn, finish, drain_three = gather(gather_two, send_sems[2], recv_sems[2])
     gather_two[0, x, z] = finish_a()
     gather_a()
-    second_turn((2,))
     gather_two[1:PARTS, x, z] = finish_b()
     gather_b()
+    second_turn((2,))
 
     lane = lax.broadcasted_iota(jnp.int32, (M, 128), 1).astype(F32)
     by_part = position_column[...].reshape(OPS, SECTORS, ROWS, 128)

time: 67.9 us -> 67.3 us (level)
  Pallas kernels: 63.9 us -> 63.2 us
where the time goes in v4:
time: 67.3 us; the launch traced here: 67.1 us
  Pallas kernels  63.2 us (94%)
  local copies, waits for them, and re-layouts  2.55 us (4%)
  between operations  1.29 us (2%)
    pallas_call x1, Pallas kernels, per_device(): pl.pallas_call(kernel, name='segment_step', out_shape=(pltpu.VMEM((OWN, M...  63.2 us
    unnamed x2, local copies, waits for them, and re-layouts  2.04 us

profile of v4, /device:TPU:8, one launch (start us, length us, event | category | flops | bytes accessed | tf_op | source)
XLA Modules:
  0.0 67.1 jit_solution(8454498279050719802)
XLA Ops:
  1.3 63.2 %segment_step.1 = (f32[24,768]{1,0:T(8,128)S(1)}, f32[8,128]{1,0:T(8,128)S(1)}, f32[768,768]{1,0:T(8,128)S(1)}) custom-call(f32[768,768]{1,0:T(8,128)} %bitcast.9, f32[768,768]{1,0:T(8,128)} %bitcast.10, f32[768,768]{1,0:T(8,128)} %bitcast.11, f32[24,768]{1,0:T(8,128)} %bitcast.12, s32[1,768]{1,0:T(1,128)} %left_charge_hbm.1, s32[1,768]{1,0:T(1,128)} %right_charge_hbm.1, ...), custom_call_target="tpu_custom_call" | custom-call | tf_op jit(solution)/shard_map/segment_step/pallas_call | solution.py:462
  64.5 0.5 slice.3
  65.0 0.6 copy.13
  65.7 1.4 %copy.14 = f32[1,1,768,768]{3,2,1,0:T(8,128)} copy(f32[1,1,768,768]{3,2,1,0:T(8,128)S(1)} %bitcast.7) | data formatting | bytes 4718592

commit v5 on v4

--- a/solution.py
+++ b/solution.py
@@ -179,13 +179,11 @@
             ref = buffer.at[0, x, z]
             for d in X_FAR:
                 send(ref, 0, 0 if d == 2 else 1, d, 0)
-            pass_a(0)
 
         def start_b():
             ref = buffer.at[1:PARTS, x, z]
             for d in Z_FAR:
                 send(ref, 1, 2 + Z_GROUP[d], 0, d)
-            pass_b(0)
 
         def turn(arrivals):
             for axis, group in arrivals:
@@ -208,7 +206,7 @@
             for at in range(4):
                 whole(at, 0).wait_send()
 
-        return start_a, start_b, turn, finish, drain
+        return start_a, start_b, pass_a, pass_b, turn, finish, drain
 
     def scatter(partial, land, sends, recvs):
         land_a, land_x, middle, land_z = land
@@ -305,9 +303,11 @@
         rows = pl.ds(p * Q, Q)
         return dot3(y_high[rows, :], y_low[rows, :], right_high[:, rows], right_low[:, rows])
 
-    start_a, start_b, turn, finish, drain_one = gather(gather_one, send_sems[0], recv_sems[0])
+    start_a, start_b, pass_a, pass_b, turn, finish, drain_one = gather(gather_one, send_sems[0], recv_sems[0])
     start_b()
     start_a()
+    pass_b(0)
+    pass_a(0)
     to_left[...] = jnp.where(place == left_place, 1.0, 0.0).astype(BF16)
     loads[3].wait()
     sort_columns(right, to_right, 0)
@@ -354,11 +354,15 @@
     turn(Z_GROUPS[2:4])
     second_turn((1,))
     turn(Z_GROUPS[4:])
-    gather_a, gather_b, turn, finish, drain_three = gather(gather_two, send_sems[2], recv_sems[2])
+    gather_a, gather_b, pass_a, pass_b, turn, finish, drain_three = gather(
+        gather_two, send_sems[2], recv_sems[2]
+    )
     gather_two[0, x, z] = finish_a()
     gather_a()
+    pass_a(0)
     gather_two[1:PARTS, x, z] = finish_b()
     gather_b()
+    pass_b(0)
     second_turn((2,))
 
     lane = lax.broadcasted_iota(jnp.int32, (M, 128), 1).astype(F32)
@@ -395,6 +399,8 @@
     start_b()
     start_a()
 
+    for drain in (drain_one, drain_two, drain_three):
+        drain()
     own_select = jnp.where(
         own_position == lax.broadcasted_iota(jnp.int32, (OWN, M), 1).astype(F32), 1.0, 0.0
     ).astype(BF16)
@@ -415,8 +421,7 @@
     )
     cheb_ref[...] = third_dot(spread_out, to_right[...], NN)
 
-    for drain in (drain_one, drain_two, drain_three, drain_four):
-        drain()
+    drain_four()
 
     @pl.when(seg < segs - 1)
     def _():

time: 67.3 us -> 67.3 us (level)
  no operation moved by 1% of the time
where the time goes in v5:
time: 67.3 us; the launch traced here: 67.1 us
  Pallas kernels  63.3 us (94%)
  local copies, waits for them, and re-layouts  2.55 us (4%)
  between operations  1.29 us (2%)
    pallas_call x1, Pallas kernels, per_device(): pl.pallas_call(kernel, name='segment_step', out_shape=(pltpu.VMEM((OWN, M...  63.3 us
    unnamed x2, local copies, waits for them, and re-layouts  2.04 us

profile of v5, /device:TPU:8, one launch (start us, length us, event | category | flops | bytes accessed | tf_op | source)
XLA Modules:
  0.0 67.1 jit_solution(5040395199310787523)
XLA Ops:
  1.3 63.3 %segment_step.1 = (f32[24,768]{1,0:T(8,128)S(1)}, f32[8,128]{1,0:T(8,128)S(1)}, f32[768,768]{1,0:T(8,128)S(1)}) custom-call(f32[768,768]{1,0:T(8,128)} %bitcast.9, f32[768,768]{1,0:T(8,128)} %bitcast.10, f32[768,768]{1,0:T(8,128)} %bitcast.11, f32[24,768]{1,0:T(8,128)} %bitcast.12, s32[1,768]{1,0:T(1,128)} %left_charge_hbm.1, s32[1,768]{1,0:T(1,128)} %right_charge_hbm.1, ...), custom_call_target="tpu_custom_call" | custom-call | tf_op jit(solution)/shard_map/segment_step/pallas_call | solution.py:467
  64.6 0.5 slice.3
  65.1 0.6 copy.13
  65.7 1.4 %copy.14 = f32[1,1,768,768]{3,2,1,0:T(8,128)} copy(f32[1,1,768,768]{3,2,1,0:T(8,128)S(1)} %bitcast.7) | data formatting | bytes 4718592
